TPU v7x, 32 devices: a whole 2x2x4 slice. The times are simulated.
32 devices in a mesh: urow: 8 (over z, core), icol: 4 (over y, x).
Axes of the slice: x: 2, y: 2, z: 4, core: 2. Of those that a mesh axis runs over, the one named last changes fastest.
Arguments:
- users: bfloat16 [8, 1024, 128], P('urow', 'icol'), may hold values from -6 to 6
- items: bfloat16 [1024, 4, 128], P('urow', 'icol'), may hold values from -6 to 6
- user_grad: bfloat16 [8, 1024, 128], P('urow', 'icol'), may hold values from -1.5 to 1.5
- item_grad: bfloat16 [1024, 4, 128], P('urow', 'icol'), may hold values from -1.5 to 1.5
- block_rows: int32 [8, 4, 12], P('urow', 'icol'), may hold values from 0 to 3, as said below
- block_cols: int32 [8, 4, 12], P('urow', 'icol'), may hold values from 0 to 3, as said below
- block_count: int32 [8, 4], P('urow', 'icol'), may hold values from 2 to 12, as said below
- block_values: bfloat16 [8, 4, 12, 256, 256], P('urow', 'icol'), may hold values from 0.0019989014 to 0.049804688
Outputs:
- user_next: bfloat16 [8, 1024, 128], P('urow', 'icol')
- item_next: bfloat16 [1024, 4, 128], P('urow', 'icol')
- user_back: bfloat16 [8, 1024, 128], P('urow', 'icol')
- item_back: bfloat16 [1024, 4, 128], P('urow', 'icol')
- value_grad: bfloat16 [8, 4, 12, 256, 256], P('urow', 'icol')
Inputs may be any that keep to these rules, and one draw needn't show every extreme that they name: `block_rows`: within one tile the 12 slots name distinct (row, column) block pairs. `block_cols`: pairs with block_rows as stated there. `block_count`: some tile has all 12 slots live in every draw.
All inputs are finite; a program needn't handle non-finite values.
Results may differ from a plain program's by a relative error of at most 0.001.
Values may be sent and summed in bfloat16 or wider, within the bound.
A program may use at most 64 MiB of HBM per device.

v0:
```python
import jax
import jax.numpy as jnp
from jax import lax
from jax.sharding import PartitionSpec as P


def shards(users, items, user_grad, item_grad, block_rows, block_cols, block_count, block_values):
    feature_dim = users.shape[2]
    slot_count = block_values.shape[2]
    block_size = block_values.shape[3]
    item_cols, item_cot = (
        lax.all_gather(items, "urow", axis=0, tiled=True),
        lax.all_gather(item_grad, "urow", axis=0, tiled=True),
    )
    user_rows, user_cot = (
        lax.all_gather(users, "icol", axis=1, tiled=True),
        lax.all_gather(user_grad, "icol", axis=1, tiled=True),
    )
    row_blocks = user_rows.shape[1] // block_size
    col_blocks = item_cols.shape[0] // block_size
    user_pair = jnp.concatenate([user_rows[0], user_cot[0]], 1).reshape(
        row_blocks, block_size, 2 * feature_dim
    )
    user_swap = jnp.concatenate([user_cot[0], user_rows[0]], 1).reshape(
        row_blocks, block_size, 2 * feature_dim
    )
    item_pair = jnp.concatenate([item_cols[:, 0], item_cot[:, 0]], 1).reshape(
        col_blocks, block_size, 2 * feature_dim
    )
    row_index = block_rows.reshape(slot_count)
    col_index = block_cols.reshape(slot_count)
    live_count = block_count.reshape(())
    tile_values = block_values.reshape(slot_count, block_size, block_size)
    live_mask = jnp.arange(slot_count, dtype=jnp.int32) < live_count
    masked = jnp.where(live_mask[:, None, None], tile_values, jnp.zeros((), tile_values.dtype))
    picked_items = item_pair[col_index]
    picked_users = user_pair[row_index]
    picked_swap = user_swap[row_index]
    user_blocks = jnp.einsum(
        "kij,kjw->kiw", masked, picked_items, preferred_element_type=jnp.float32
    )
    item_blocks = jnp.einsum(
        "kij,kiw->kjw", masked, picked_users, preferred_element_type=jnp.float32
    )
    row_hot = (row_index[:, None] == jnp.arange(row_blocks, dtype=jnp.int32)[None, :]).astype(
        jnp.float32
    )
    col_hot = (col_index[:, None] == jnp.arange(col_blocks, dtype=jnp.int32)[None, :]).astype(
        jnp.float32
    )
    user_part = jnp.einsum("ku,kiw->uiw", row_hot, user_blocks, precision=lax.Precision.HIGHEST)
    item_part = jnp.einsum("ku,kiw->uiw", col_hot, item_blocks, precision=lax.Precision.HIGHEST)
    grads = jnp.einsum(
        "kiw,kjw->kij", picked_swap, picked_items, preferred_element_type=jnp.float32
    )
    grads = jnp.where(live_mask[:, None, None], grads, 0.0).astype(jnp.bfloat16)
    user_flat = user_part.reshape(row_blocks * block_size, 2 * feature_dim)
    item_flat = item_part.reshape(col_blocks * block_size, 2 * feature_dim)
    user_whole = user_flat.reshape(1, row_blocks * block_size, 2 * feature_dim)
    item_whole = item_flat.reshape(col_blocks * block_size, 1, 2 * feature_dim)
    user_fwd, user_bwd = (
        lax.psum_scatter(user_whole[:, :, :feature_dim], "icol", scatter_dimension=1, tiled=True),
        lax.psum_scatter(user_whole[:, :, feature_dim:], "icol", scatter_dimension=1, tiled=True),
    )
    item_fwd, item_bwd = (
        lax.psum_scatter(item_whole[:, :, :feature_dim], "urow", scatter_dimension=0, tiled=True),
        lax.psum_scatter(item_whole[:, :, feature_dim:], "urow", scatter_dimension=0, tiled=True),
    )
    return (
        user_fwd.astype(jnp.bfloat16),
        item_fwd.astype(jnp.bfloat16),
        user_bwd.astype(jnp.bfloat16),
        item_bwd.astype(jnp.bfloat16),
        grads.reshape(1, 1, slot_count, block_size, block_size),
    )


def solution(mesh):
    in_specs = (
        P("urow", "icol", None),
        P("urow", "icol", None),
        P("urow", "icol", None),
        P("urow", "icol", None),
        P("urow", "icol", None),
        P("urow", "icol", None),
        P("urow", "icol"),
        P("urow", "icol", None, None, None),
    )
    out_specs = (
        P("urow", "icol", None),
        P("urow", "icol", None),
        P("urow", "icol", None),
        P("urow", "icol", None),
        P("urow", "icol", None, None, None),
    )
    return jax.shard_map(shards, mesh=mesh, in_specs=in_specs, out_specs=out_specs, check_vma=False)
```

profile of v0, /device:TPU:0, one launch (start us, length us, event | category | flops | bytes accessed | tf_op | source)
XLA Modules:
  0.0 161.4 jit_solution(15094072141230355249)
XLA Ops:
  7.2 0.0 reduce-scatter.7.cloned.1.call-start
  7.2 10.7 %all_gather.14 = bf16[1,1024,128]{2,1,0:T(8,128)(2,1)S(1)} all-gather(bf16[1,256,128]{2,1,0:T(8,128)(2,1)} %param.8), channel_id=1, replica_groups=mesh['urow'=8,'icol'=4] {'icol'}, dimensions={1}, use_global_device_ids=true | all-gather | bytes 327680 | tf_op jit(solution)/shard_map/all_gather | solution.py:16
  17.9 8.7 %all_gather.15 = bf16[1,1024,128]{2,1,0:T(8,128)(2,1)S(1)} all-gather(bf16[1,256,128]{2,1,0:T(8,128)(2,1)} %param.10), channel_id=1, replica_groups=mesh['urow'=8,'icol'=4] {'icol'}, dimensions={1}, use_global_device_ids=true | all-gather | bytes 327680 | tf_op jit(solution)/shard_map/all_gather | solution.py:17
  26.6 0.7 fusion.14
  28.0 0.1 pad_maximum_fusion.2
  28.0 0.0 copy-start
  28.0 1.8 %gather_fusion.1 = bf16[12,256,256]{2,1,0:T(8,128)(2,1)} fusion(bf16[4,256,256]{2,1,0:T(8,128)(2,1)S(1)} %get-tuple-element.10, s32[1024]{0:T(1024)S(1)} %pad_clamp_fusion), kind=kCustom, calls=%fused_computation.1 | custom fusion | bytes 3145776 | tf_op jit(solution)/shard_map/gather | solution.py:37
  29.9 0.0 copy-done
  29.9 0.0 copy-start.4
  29.9 2.1 %fusion.5 = f32[12,256,256]{2,1,0:T(8,128)S(1)} fusion(bf16[12,256,256]{2,1,0:T(8,128)(2,1)} %gather_fusion.1, bf16[1,1,12,256,256]{4,3,2,1,0:T(8,128)(2,1)S(1)} %copy-done, pred[12]{0:T(512)(128)(4,1)S(1)} %iota_compare_fusion.2), kind=kOutput, calls=%fused_computation.10 | convolution fusion | flops 403439616 | bytes 6291468 | tf_op jit(solution)/shard_map/kij,kiw->kjw/dot_general | solution.py:42
  32.0 0.0 copy-done.4
  32.0 3.3 %fusion = f32[4,256,256]{2,0,1:T(4,128)S(1)} fusion(f32[12,256,256]{2,1,0:T(8,128)S(1)} %fusion.5, s32[12]{0:T(128)S(1)} %bitcast.40), kind=kOutput, calls=%fused_computation.3 | convolution fusion | flops 37748784 | bytes 4194352 | tf_op jit(solution)/shard_map/ku,kiw->uiw/dot_general | solution.py:52
  35.3 0.2 copy.14
  35.5 0.0 copy-start.2
  35.5 0.0 copy-start.3
  35.5 1.0 fusion.17
  36.6 0.0 reduce-scatter.7.cloned.1.call-update
  36.6 0.0 reduce-scatter.11.cloned.1.call-start
  36.6 0.7 reduce-scatter.11.cloned.1.call-update
  37.3 0.0 reduce-scatter.5.cloned.1.call-start
  37.4 0.0 copy-done.2
  37.4 14.5 %all_gather.12 = bf16[1024,1,128]{2,0,1:T(8,128)(2,1)S(1)} all-gather(bf16[128,1,128]{2,0,1:T(8,128)(2,1)S(1)} %copy-done.2), channel_id=1, replica_groups=mesh['urow'=8,'icol'=4] {'urow'}, dimensions={0}, use_global_device_ids=true | all-gather | bytes 294912 | tf_op jit(solution)/shard_map/all_gather | solution.py:12
  51.9 0.0 copy-done.3
  51.9 15.1 %all_gather.13 = bf16[1024,1,128]{2,0,1:T(8,128)(2,1)S(1)} all-gather(bf16[128,1,128]{2,0,1:T(8,128)(2,1)S(1)} %copy-done.3), channel_id=1, replica_groups=mesh['urow'=8,'icol'=4] {'urow'}, dimensions={0}, use_global_device_ids=true | all-gather | bytes 294912 | tf_op jit(solution)/shard_map/all_gather | solution.py:13
  67.0 0.1 pad_maximum_fusion
  67.0 1.8 %gather_fusion = bf16[12,256,256]{2,1,0:T(8,128)(2,1)} fusion(bf16[4,256,256]{2,1,0:T(8,128)(2,1)S(1)} %pad_maximum_fusion, s32[1024]{0:T(1024)S(1)} %pad_clamp_fusion.1), kind=kCustom, calls=%fused_computation | custom fusion | bytes 3145776 | tf_op jit(solution)/shard_map/gather | solution.py:36
  68.9 0.0 copy-start.5
  68.9 2.0 %fusion.6 = f32[12,256,256]{2,1,0:T(8,128)S(1)} fusion(bf16[12,256,256]{2,1,0:T(8,128)(2,1)} %gather_fusion, bf16[1,1,12,256,256]{4,3,2,1,0:T(8,128)(2,1)S(1)} %copy-done, pred[12]{0:T(512)(128)(4,1)S(1)} %iota_compare_fusion.2), kind=kOutput, calls=%fused_computation.11 | convolution fusion | flops 403439616 | bytes 6291468 | tf_op jit(solution)/shard_map/kij,kjw->kiw/dot_general | solution.py:39
  70.9 0.0 copy-done.5
  70.9 3.2 %fusion.2 = f32[4,256,256]{2,0,1:T(4,128)S(1)} fusion(f32[12,256,256]{2,1,0:T(8,128)S(1)} %fusion.6, s32[12]{0:T(128)S(1)} %bitcast.41), kind=kOutput, calls=%fused_computation.5 | convolution fusion | flops 37748784 | bytes 4194352 | tf_op jit(solution)/shard_map/ku,kiw->uiw/dot_general | solution.py:51
  74.2 0.2 copy.13
  74.4 1.0 fusion.18
  75.5 0.0 reduce-scatter.5.cloned.1.call-update
  75.5 0.0 reduce-scatter.9.cloned.1.call-start
  75.5 0.5 reduce-scatter.9.cloned.1.call-update
  76.1 0.0 copy-start.1
  76.1 1.8 %gather_fusion.2 = bf16[12,256,256]{2,1,0:T(8,128)(2,1)} fusion(bf16[4,256,256]{2,1,0:T(8,128)(2,1)S(1)} %get-tuple-element.9, s32[1024]{0:T(1024)S(1)} %pad_clamp_fusion), kind=kCustom, calls=%fused_computation.2 | custom fusion | bytes 3145776 | tf_op jit(solution)/shard_map/gather | solution.py:38
  77.9 0.0 copy-done.1
  77.9 3.2 %fusion.4 = bf16[1,1,12,256,256]{4,3,2,1,0:T(8,128)(2,1)} fusion(bf16[12,256,256]{2,1,0:T(8,128)(2,1)} %gather_fusion.2, bf16[12,256,256]{2,1,0:T(8,128)(2,1)S(1)} %copy-done.1, pred[12]{0:T(512)(128)(4,1)S(1)} %iota_compare_fusion.2), kind=kOutput, calls=%fused_computation.9 | convolution fusion | flops 404226048 | bytes 4718604 | tf_op jit(solution)/shard_map/kiw,kjw->kij/dot_general | solution.py:53
  81.1 0.0 reduce-scatter.7.cloned.1.call-done
  81.1 1.5 convert_element_type.18
  82.5 17.2 %reduce-scatter.11.cloned.1.call-done = f32[128,1,128]{2,0,1:T(8,128)} async-done(((f32[1024,1,128]{2,0,1:T(8,128)}), f32[128,1,128]{2,0,1:T(8,128)}) %reduce-scatter.11.cloned.1.call-update) | async-done | bytes 65552 | tf_op jit(solution)/shard_map/reduce_scatter | solution.py:67
  99.8 1.5 convert_element_type.20
  101.2 24.4 %reduce-scatter.5.cloned.1.call-done = f32[1,256,128]{2,1,0:T(8,128)} async-done(((f32[1,1024,128]{2,1,0:T(8,128)}), f32[1,256,128]{2,1,0:T(8,128)}) %reduce-scatter.5.cloned.1.call-update) | async-done | bytes 131088 | tf_op jit(solution)/shard_map/reduce_scatter | solution.py:62
  125.7 1.5 convert_element_type.17
  127.2 26.2 %reduce-scatter.9.cloned.1.call-done = f32[1,256,128]{2,1,0:T(8,128)} async-done(((f32[1,1024,128]{2,1,0:T(8,128)}), f32[1,256,128]{2,1,0:T(8,128)}) %reduce-scatter.9.cloned.1.call-update) | async-done | bytes 131088 | tf_op jit(solution)/shard_map/reduce_scatter | solution.py:63
  153.4 1.5 convert_element_type.19
  (4 shorter events, 0.0 us)
Async XLA Ops:
  7.2 73.9 %reduce-scatter.7.cloned.1.call-start = ((), (), s32[]{:S(2)}) async-start(), calls=%async_computation.5 | async-start | bytes 589824 | tf_op jit(solution)/shard_map/reduce_scatter | solution.py:66
  28.0 1.9 %copy-start = (bf16[1,1,12,256,256]{4,3,2,1,0:T(8,128)(2,1)S(1)}, bf16[1,1,12,256,256]{4,3,2,1,0:T(8,128)(2,1)}, u32[]{:S(2)}) copy-start(bf16[1,1,12,256,256]{4,3,2,1,0:T(8,128)(2,1)} %param.15) | copy-start | bytes 4718596
  29.9 2.1 %copy-start.4 = (s32[1,1,12]{2,1,0:T(1,128)S(1)}, s32[1,1,12]{2,1,0:T(1,128)}, u32[]{:S(2)}) copy-start(s32[1,1,12]{2,1,0:T(1,128)} %param.13) | copy-start | bytes 148
  35.5 1.9 %copy-start.2 = (bf16[128,1,128]{2,0,1:T(8,128)(2,1)S(1)}, bf16[128,1,128]{2,0,1:T(8,128)(2,1)}, u32[]{:S(2)}) copy-start(bf16[128,1,128]{2,0,1:T(8,128)(2,1)} %param.9) | copy-start | bytes 98308
  35.5 16.4 %copy-start.3 = (bf16[128,1,128]{2,0,1:T(8,128)(2,1)S(1)}, bf16[128,1,128]{2,0,1:T(8,128)(2,1)}, u32[]{:S(2)}) copy-start(bf16[128,1,128]{2,0,1:T(8,128)(2,1)} %param.11) | copy-start | bytes 98308
  36.6 63.2 %reduce-scatter.11.cloned.1.call-start = ((), (), s32[]{:S(2)}) async-start(), calls=%async_computation.7 | async-start | bytes 589824 | tf_op jit(solution)/shard_map/reduce_scatter | solution.py:67
  37.3 88.3 %reduce-scatter.5.cloned.1.call-start = ((), (), s32[]{:S(2)}) async-start(), calls=%async_computation.4 | async-start | bytes 655360 | tf_op jit(solution)/shard_map/reduce_scatter | solution.py:62
  68.9 2.0 %copy-start.5 = (s32[1,1,12]{2,1,0:T(1,128)S(1)}, s32[1,1,12]{2,1,0:T(1,128)}, u32[]{:S(2)}) copy-start(s32[1,1,12]{2,1,0:T(1,128)} %param.12) | copy-start | bytes 148
  75.5 77.9 %reduce-scatter.9.cloned.1.call-start = ((), (), s32[]{:S(2)}) async-start(), calls=%async_computation.6 | async-start | bytes 655360 | tf_op jit(solution)/shard_map/reduce_scatter | solution.py:63
  76.1 1.9 %copy-start.1 = (bf16[12,256,256]{2,1,0:T(8,128)(2,1)S(1)}, bf16[12,256,256]{2,1,0:T(8,128)(2,1)}, u32[]{:S(2)}) copy-start(bf16[12,256,256]{2,1,0:T(8,128)(2,1)} %gather_fusion) | copy-start | bytes 4718596
Sparse Core Ops, SparseCore 0:
  36.7 31.1 reduce-scatter.6
  70.3 29.4 reduce-scatter.10
  102.6 23.0 reduce-scatter.4
  128.6 24.7 reduce-scatter.8
where the time goes:
time: 162 us; the launch traced here: 161 us
  waiting for transfers between devices  69.1 us (43%)
  blocking collectives  49 us (30%)
  between operations  14.6 us (9%)
  matrix products  13.8 us (9%)
  local copies, waits for them, and re-layouts  8.05 us (5%)
  other arithmetic  6.81 us (4%)
    reduce_scatter x1, waiting for transfers between devices, shards(): lax.psum_scatter(user_whole[:, :, feature_dim:], 'icol', scatter_dimensio...  26.2 us
    reduce_scatter x1, waiting for transfers between devices, shards(): lax.psum_scatter(user_whole[:, :, :feature_dim], 'icol', scatter_dimensio...  24.4 us
    reduce_scatter x1, waiting for transfers between devices, shards(): lax.psum_scatter(item_whole[:, :, feature_dim:], 'urow', scatter_dimensio...  17.2 us
    all_gather x1, blocking collectives, shards(): lax.all_gather(item_grad, 'urow', axis=0, tiled=True)  15.1 us
    all_gather x1, blocking collectives, shards(): lax.all_gather(items, 'urow', axis=0, tiled=True)  14.5 us
    all_gather x1, blocking collectives, shards(): lax.all_gather(users, 'icol', axis=1, tiled=True)  10.7 us
    all_gather x1, blocking collectives, shards(): lax.all_gather(user_grad, 'icol', axis=1, tiled=True)  8.68 us
    dot_general x1, matrix products, shards(): jnp.einsum('ku,kiw->uiw', col_hot, item_blocks, precision=lax.Precision.H...  3.25 us
  transfers between devices with their start and end apart: 4, of which 3 were waited for; matrix products, arithmetic and copies ran while one was open for 11% of the time, Pallas kernels for 0%

commit v1 on v0

v1 whole, which is shorter than its diff:
```python
import functools

import jax
import jax.numpy as jnp
from jax import lax
from jax.experimental import pallas as pl
from jax.experimental.pallas import tpu as pltpu
from jax.sharding import PartitionSpec as P

MESH = pl.DeviceIdType.MESH


def kernel(
    n_urow, n_icol, users, items, user_grad, item_grad, rows, cols, count, values,
    user_next, item_next, user_back, item_back, grads_out,
    upair, ipair, blocks, dense, dense_t, upart, ipart, csum, pbuf, rbuf_i, rbuf_u, grads,
    local_sem, value_sem, grad_sem, su, ru, si, ri, sf, rf, sp, rp, sx, rx, sc, rc,
):
    width = users.shape[1]
    ru_rows, ri_rows = users.shape[0], items.shape[0]
    slots, size = values.shape[0], values.shape[1]
    ub, ib = upair.shape[0], ipair.shape[0]
    chips = n_urow // 2
    me_u, me_i = lax.axis_index("urow"), lax.axis_index("icol")
    core, chip = lax.rem(me_u, 2), me_u // 2
    partner = me_u + 1 - 2 * core

    def urows(index):
        return pl.ds(pl.multiple_of(index * ru_rows, ru_rows), ru_rows)

    def irows(index):
        return pl.ds(pl.multiple_of(index * ri_rows, ri_rows), ri_rows)

    def in_pair(index, count):
        start = index * count
        return start // size, pl.ds(pl.multiple_of(lax.rem(start, size), count), count)

    def upart_of(index):
        return upair.at[in_pair(index, ru_rows)]

    def ipart_of(index):
        return ipair.at[in_pair(index, ri_rows)]

    def remote(src, dst, send, recv, where):
        return pltpu.make_async_remote_copy(
            src_ref=src, dst_ref=dst, send_sem=send, recv_sem=recv,
            device_id=where, device_id_type=MESH,
        )

    chip_peers = [lax.rem(chip + o, chips) for o in range(1, chips)]
    icol_peers = [lax.rem(me_i + o, n_icol) for o in range(1, n_icol)]

    lo, hi = pl.ds(0, width), pl.ds(width, width)
    local = [
        pltpu.make_async_copy(items, ipair.at[(*in_pair(me_u, ri_rows), lo)], local_sem.at[0]),
        pltpu.make_async_copy(item_grad, ipair.at[(*in_pair(me_u, ri_rows), hi)], local_sem.at[1]),
        pltpu.make_async_copy(users, upair.at[(*in_pair(me_i, ru_rows), lo)], local_sem.at[2]),
        pltpu.make_async_copy(user_grad, upair.at[(*in_pair(me_i, ru_rows), hi)], local_sem.at[3]),
    ]
    for copy in local:
        copy.start()
    value_copy = pltpu.make_async_copy(values, blocks, value_sem)
    value_copy.start()

    barrier = pltpu.get_barrier_semaphore()
    pl.semaphore_signal(barrier, inc=1, device_id={"urow": partner}, device_id_type=MESH)
    for g in chip_peers:
        pl.semaphore_signal(barrier, inc=1, device_id={"urow": 2 * g + core}, device_id_type=MESH)
    for j in icol_peers:
        pl.semaphore_signal(barrier, inc=1, device_id={"icol": j}, device_id_type=MESH)
    pl.semaphore_wait(barrier, 1 + len(chip_peers) + len(icol_peers))
    for copy in local:
        copy.wait()

    mine_i, mine_u = ipart_of(me_u), upart_of(me_i)
    sends = []
    for g in chip_peers:
        sends.append(remote(mine_i, mine_i, si.at[g], ri.at[chip], {"urow": 2 * g + core}))
    for j in icol_peers:
        sends.append(remote(mine_u, mine_u, su.at[j], ru.at[me_i], {"icol": j}))
    sends.append(remote(mine_i, mine_i, sf.at[chip], rf.at[chip], {"urow": partner}))
    for copy in sends:
        copy.start()

    value_copy.wait()
    live_count = count[0, 0]
    for u in range(ub):
        for c in range(ib):
            slot, live = jnp.int32(0), jnp.float32(0.0)
            for k in range(slots):
                hit = (rows[0, 0, k] == u) & (cols[0, 0, k] == c) & (k < live_count)
                slot = jnp.where(hit, k, slot)
                live = jnp.where(hit, jnp.float32(1.0), live)
            block = (blocks[slot].astype(jnp.float32) * live).astype(jnp.bfloat16)
            dense[u * size:(u + 1) * size, c * size:(c + 1) * size] = block
            dense_t[c * size:(c + 1) * size, u * size:(u + 1) * size] = block.T

    for g in chip_peers:
        there = ipart_of(2 * g + core)
        remote(mine_i, there, si.at[g], ri.at[g], {"urow": partner}).wait_recv()
        copy = remote(there, there, sf.at[g], rf.at[g], {"urow": partner})
        copy.start()
        sends.append(copy)

    for j in icol_peers:
        remote(mine_u, upart_of(j), su.at[j], ru.at[j], {"icol": j}).wait_recv()
    for c in range(ib):
        at = slice(c * size, (c + 1) * size)
        ipart[at] = jnp.dot(dense_t[at], upair[...].reshape(-1, 2 * width), preferred_element_type=jnp.float32)
    for g in chip_peers + [chip]:
        copy = remote(
            ipart.at[irows(2 * g + 1 - core)], pbuf.at[g], sp.at[g], rp.at[g], {"urow": partner}
        )
        copy.start()
        sends.append(copy)

    for g in [chip] + chip_peers:
        there = ipart_of(2 * g + 1 - core)
        remote(there, there, sf.at[g], rf.at[g], {"urow": partner}).wait_recv()
    for u in range(ub):
        at = slice(u * size, (u + 1) * size)
        upart[at] = jnp.dot(dense[at], ipair[...].reshape(-1, 2 * width), preferred_element_type=jnp.float32)
    for j in icol_peers:
        copy = remote(upart.at[urows(j)], rbuf_u.at[me_i], sx.at[j], rx.at[me_i], {"icol": j})
        copy.start()
        sends.append(copy)

    for g in chip_peers + [chip]:
        remote(pbuf.at[g], pbuf.at[g], sp.at[g], rp.at[g], {"urow": partner}).wait_recv()
    for g in chip_peers:
        csum[g] = ipart[irows(2 * g + core)] + pbuf[g]
        copy = remote(csum.at[g], rbuf_i.at[chip], sc.at[g], rc.at[chip], {"urow": 2 * g + core})
        copy.start()
        sends.append(copy)

    writes = []
    for k in range(slots):
        left = upair[rows[0, 0, k]]
        right = ipair[cols[0, 0, k]]
        swap = jnp.concatenate([left[:, width:], left[:, :width]], 1)
        grad = lax.dot_general(
            swap, right, (((1,), (1,)), ((), ())), preferred_element_type=jnp.float32
        )
        grads[k] = jnp.where(k < live_count, grad, 0.0).astype(jnp.bfloat16)
        copy = pltpu.make_async_copy(grads.at[k], grads_out.at[k], grad_sem.at[k])
        copy.start()
        writes.append(copy)

    total = ipart[irows(me_u)] + pbuf[chip]
    for g in chip_peers:
        remote(csum.at[g], rbuf_i.at[g], sc.at[g], rc.at[g], {"urow": partner}).wait_recv()
        total = total + rbuf_i[g]
    item_next[...] = total[:, :width].astype(jnp.bfloat16)
    item_back[...] = total[:, width:].astype(jnp.bfloat16)
    total = upart[urows(me_i)]
    for j in icol_peers:
        remote(upart.at[urows(j)], rbuf_u.at[j], sx.at[j], rx.at[j], {"icol": j}).wait_recv()
        total = total + rbuf_u[j]
    user_next[...] = total[:, :width].astype(jnp.bfloat16)
    user_back[...] = total[:, width:].astype(jnp.bfloat16)
    for copy in writes:
        copy.wait()
    for copy in sends:
        copy.wait_send()


def shards(n_urow, n_icol, users, items, user_grad, item_grad, block_rows, block_cols, block_count, block_values):
    width = users.shape[2]
    ru_rows, ri_rows = users.shape[1], items.shape[0]
    slots, size = block_values.shape[2], block_values.shape[3]
    all_u, all_i = ru_rows * n_icol, ri_rows * n_urow
    chips = n_urow // 2
    bf16, f32 = jnp.bfloat16, jnp.float32
    hbm = pl.BlockSpec(memory_space=pl.ANY)
    smem = pl.BlockSpec(memory_space=pltpu.SMEM)
    vmem = pl.BlockSpec(memory_space=pltpu.VMEM)
    dma = pltpu.SemaphoreType.DMA
    un, in_, ub, ib, grads = pl.pallas_call(
        functools.partial(kernel, n_urow, n_icol),
        out_shape=(
            jax.ShapeDtypeStruct((ru_rows, width), bf16),
            jax.ShapeDtypeStruct((ri_rows, width), bf16),
            jax.ShapeDtypeStruct((ru_rows, width), bf16),
            jax.ShapeDtypeStruct((ri_rows, width), bf16),
            jax.ShapeDtypeStruct((slots, size, size), bf16),
        ),
        in_specs=[hbm] * 4 + [smem] * 3 + [hbm],
        out_specs=(vmem, vmem, vmem, vmem, hbm),
        scratch_shapes=[
            pltpu.VMEM((all_u // size, size, 2 * width), bf16),
            pltpu.VMEM((all_i // size, size, 2 * width), bf16),
            pltpu.VMEM((slots, size, size), bf16),
            pltpu.VMEM((all_u, all_i), bf16),
            pltpu.VMEM((all_i, all_u), bf16),
            pltpu.VMEM((all_u, 2 * width), f32),
            pltpu.VMEM((all_i, 2 * width), f32),
            pltpu.VMEM((chips, ri_rows, 2 * width), f32),
            pltpu.VMEM((chips, ri_rows, 2 * width), f32),
            pltpu.VMEM((chips, ri_rows, 2 * width), f32),
            pltpu.VMEM((n_icol, ru_rows, 2 * width), f32),
            pltpu.VMEM((slots, size, size), bf16),
            dma((4,)), dma, dma((slots,)),
            dma((n_icol,)), dma((n_icol,)), dma((chips,)), dma((chips,)),
            dma((chips,)), dma((chips,)), dma((chips,)), dma((chips,)),
            dma((n_icol,)), dma((n_icol,)), dma((chips,)), dma((chips,)),
        ],
        compiler_params=pltpu.CompilerParams(
            collective_id=0, has_side_effects=True, vmem_limit_bytes=63 * 1024 * 1024
        ),
    )(
        users.reshape(ru_rows, width), items.reshape(ri_rows, width),
        user_grad.reshape(ru_rows, width), item_grad.reshape(ri_rows, width),
        block_rows, block_cols, block_count, block_values.reshape(slots, size, size),
    )
    return (
        un.reshape(1, ru_rows, width), in_.reshape(ri_rows, 1, width),
        ub.reshape(1, ru_rows, width), ib.reshape(ri_rows, 1, width),
        grads.reshape(1, 1, slots, size, size),
    )


def solution(mesh):
    body = functools.partial(shards, mesh.shape["urow"], mesh.shape["icol"])
    row = P("urow", "icol", None)
    return jax.shard_map(
        body,
        mesh=mesh,
        in_specs=(row, row, row, row, row, row, P("urow", "icol"), P("urow", "icol", None, None, None)),
        out_specs=(row, row, row, row, P("urow", "icol", None, None, None)),
        check_vma=False,
    )
```

time: 162 us -> 38.8 us (0.24)
  waiting for transfers between devices: 69.1 us -> 0 us
  blocking collectives: 49 us -> 0 us
  Pallas kernels: 0 us -> 28.8 us
  matrix products: 13.8 us -> 0 us
  between operations: 14.6 us -> 1.29 us
  other arithmetic: 6.81 us -> 0 us
    reduce_scatter x4 -> x0, waiting for transfers between devices: 67.8 us -> none  [the longest x1 26.2 us: shards(): lax.psum_scatter(user_whole[:, :, feature_dim:], 'icol', scatter_dimensio...]
    all_gather x4 -> x0, blocking collectives: 49 us -> none  [the longest x1 15.1 us: shards(): lax.all_gather(item_grad, 'urow', axis=0, tiled=True)]
    pallas_call x0 -> x1, Pallas kernels: none -> 28.8 us  [shards(): pl.pallas_call(functools.partial(kernel, n_urow, n_icol), out_shape=(jax....]
    dot_general x5 -> x0, matrix products: 13.8 us -> none  [the longest x1 3.25 us: shards(): jnp.einsum('ku,kiw->uiw', col_hot, item_blocks, precision=lax.Precision.H...]
    unnamed x12 -> x5, local copies, waits for them, and re-layouts: 0.03 us -> 8.34 us
    convert_element_type x4 -> x0, other arithmetic: 6 us -> none  [the longest x1 1.54 us: shards(): user_fwd.astype(jnp.bfloat16)]
    gather x3 -> x0, local copies, waits for them, and re-layouts: 5.53 us -> none  [the longest x1 1.84 us: shards(): picked_swap = user_swap[row_index]]
    slice x2 -> x0, local copies, waits for them, and re-layouts: 2.08 us -> none  [the longest x1 1.04 us: shards(): user_whole[:, :, feature_dim:]]
  transfers between devices with their start and end apart: 4 -> 0, of which waited for: 3 -> 0; matrix products, arithmetic and copies ran while one was open for 11% -> 0% of each run, Pallas kernels for 0% -> 0%
where the time goes in v1:
time: 38.8 us; the launch traced here: 38.4 us
  Pallas kernels  28.8 us (74%)
  local copies, waits for them, and re-layouts  8.34 us (21%)
  between operations  1.29 us (3%)
    pallas_call x1, Pallas kernels, shards(): pl.pallas_call(functools.partial(kernel, n_urow, n_icol), out_shape=(jax....  28.8 us
    unnamed x5, local copies, waits for them, and re-layouts  8.34 us

profile of v1, /device:TPU:0, one launch (start us, length us, event | category | flops | bytes accessed | tf_op | source)
XLA Modules:
  0.0 38.4 jit_solution(4357485749275304222)
XLA Ops:
  1.3 28.8 %shard_map.119 = (bf16[256,128]{1,0:T(8,128)(2,1)}, bf16[128,128]{1,0:T(8,128)(2,1)}, bf16[256,128]{1,0:T(8,128)(2,1)}, bf16[128,128]{1,0:T(8,128)(2,1)}, bf16[12,256,256]{2,1,0:T(8,128)(2,1)}) custom-call(bf16[256,128]{1,0:T(8,128)(2,1)} %bitcast.12, bf16[128,128]{1,0:T(8,128)(2,1)} %bitcast.16, bf16[256,128]{1,0:T(8,128)(2,1)} %bitcast.13, ...), custom_call_target="tpu_custom_call" | custom-call | tf_op jit(solution)/shard_map/pallas_call | solution.py:178
  30.0 1.5 %copy.19 = bf16[1,256,128]{2,1,0:T(8,128)(2,1)} copy(bf16[1,256,128]{2,1,0:T(8,128)(2,1)} %bitcast.15) | data formatting | bytes 131072
  31.5 1.4 %copy.20 = bf16[128,1,128]{2,0,1:T(8,128)(2,1)} copy(bf16[128,1,128]{2,0,1:T(8,128)(2,1)} %bitcast.19) | data formatting | bytes 65536
  32.9 1.5 %copy.21 = bf16[1,256,128]{2,1,0:T(8,128)(2,1)} copy(bf16[1,256,128]{2,1,0:T(8,128)(2,1)} %bitcast.14) | data formatting | bytes 131072
  34.4 1.4 %copy.22 = bf16[128,1,128]{2,0,1:T(8,128)(2,1)} copy(bf16[128,1,128]{2,0,1:T(8,128)(2,1)} %bitcast.18) | data formatting | bytes 65536
  35.7 2.7 %copy.23 = bf16[1,1,12,256,256]{4,3,2,1,0:T(8,128)(2,1)} copy(bf16[1,1,12,256,256]{4,3,2,1,0:T(8,128)(2,1)} %bitcast.11) | data formatting | bytes 3145728

commit v2 on v1

--- a/solution.py
+++ b/solution.py
@@ -10,10 +10,39 @@
 MESH = pl.DeviceIdType.MESH
 
 
+LEVELS = 32766.0
+STEPS = 88.0
+EXTRA = 16
+
+
+def encode(sums, coded):
+    count = sums.shape[0]
+    top = jnp.maximum(jnp.max(jnp.abs(sums), axis=0, keepdims=True), 1e-30)
+    level = jnp.floor(jnp.log(top) * STEPS) + 2.0
+    coded[:count] = jnp.round(sums * (jnp.exp(level * (-1.0 / STEPS)) * LEVELS)).astype(jnp.int32).astype(jnp.int16)
+    level = jnp.broadcast_to(level, (EXTRA, sums.shape[1]))
+    coded[count:] = level.astype(jnp.int32).astype(jnp.int16)
+
+
+def decode(coded):
+    count = coded.shape[0] - EXTRA
+    level = coded[count:].astype(jnp.int32).astype(jnp.float32)[:1]
+    return coded[:count].astype(jnp.int32).astype(jnp.float32) * (jnp.exp(level * (1.0 / STEPS)) * (1.0 / LEVELS))
+
+
+def hand_over(*refs):
+    half = (len(refs) - 1) // 2
+    copies = [pltpu.make_async_copy(refs[i], refs[half + i], refs[-1].at[i]) for i in range(half)]
+    for copy in copies:
+        copy.start()
+    for copy in copies:
+        copy.wait()
+
+
 def kernel(
     n_urow, n_icol, users, items, user_grad, item_grad, rows, cols, count, values,
     user_next, item_next, user_back, item_back, grads_out,
-    upair, ipair, blocks, dense, dense_t, upart, ipart, csum, pbuf, rbuf_i, rbuf_u, grads,
+    upair, ipair, blocks, dense, dense_t, upart, ipart, csum, pbuf, sbuf_u, rbuf_i, rbuf_u, grads,
     local_sem, value_sem, grad_sem, su, ru, si, ri, sf, rf, sp, rp, sx, rx, sc, rc,
 ):
     width = users.shape[1]
@@ -121,14 +150,15 @@
         at = slice(u * size, (u + 1) * size)
         upart[at] = jnp.dot(dense[at], ipair[...].reshape(-1, 2 * width), preferred_element_type=jnp.float32)
     for j in icol_peers:
-        copy = remote(upart.at[urows(j)], rbuf_u.at[me_i], sx.at[j], rx.at[me_i], {"icol": j})
+        encode(upart[urows(j)], sbuf_u.at[j])
+        copy = remote(sbuf_u.at[j], rbuf_u.at[me_i], sx.at[j], rx.at[me_i], {"icol": j})
         copy.start()
         sends.append(copy)
 
     for g in chip_peers + [chip]:
         remote(pbuf.at[g], pbuf.at[g], sp.at[g], rp.at[g], {"urow": partner}).wait_recv()
     for g in chip_peers:
-        csum[g] = ipart[irows(2 * g + core)] + pbuf[g]
+        encode(ipart[irows(2 * g + core)] + pbuf[g], csum.at[g])
         copy = remote(csum.at[g], rbuf_i.at[chip], sc.at[g], rc.at[chip], {"urow": 2 * g + core})
         copy.start()
         sends.append(copy)
@@ -149,13 +179,13 @@
     total = ipart[irows(me_u)] + pbuf[chip]
     for g in chip_peers:
         remote(csum.at[g], rbuf_i.at[g], sc.at[g], rc.at[g], {"urow": partner}).wait_recv()
-        total = total + rbuf_i[g]
+        total = total + decode(rbuf_i.at[g])
     item_next[...] = total[:, :width].astype(jnp.bfloat16)
     item_back[...] = total[:, width:].astype(jnp.bfloat16)
     total = upart[urows(me_i)]
     for j in icol_peers:
-        remote(upart.at[urows(j)], rbuf_u.at[j], sx.at[j], rx.at[j], {"icol": j}).wait_recv()
-        total = total + rbuf_u[j]
+        remote(sbuf_u.at[j], rbuf_u.at[j], sx.at[j], rx.at[j], {"icol": j}).wait_recv()
+        total = total + decode(rbuf_u.at[j])
     user_next[...] = total[:, :width].astype(jnp.bfloat16)
     user_back[...] = total[:, width:].astype(jnp.bfloat16)
     for copy in writes:
@@ -175,7 +205,7 @@
     smem = pl.BlockSpec(memory_space=pltpu.SMEM)
     vmem = pl.BlockSpec(memory_space=pltpu.VMEM)
     dma = pltpu.SemaphoreType.DMA
-    un, in_, ub, ib, grads = pl.pallas_call(
+    results = pl.pallas_call(
         functools.partial(kernel, n_urow, n_icol),
         out_shape=(
             jax.ShapeDtypeStruct((ru_rows, width), bf16),
@@ -194,10 +224,11 @@
             pltpu.VMEM((all_i, all_u), bf16),
             pltpu.VMEM((all_u, 2 * width), f32),
             pltpu.VMEM((all_i, 2 * width), f32),
+            pltpu.VMEM((chips, ri_rows + EXTRA, 2 * width), jnp.int16),
             pltpu.VMEM((chips, ri_rows, 2 * width), f32),
-            pltpu.VMEM((chips, ri_rows, 2 * width), f32),
-            pltpu.VMEM((chips, ri_rows, 2 * width), f32),
-            pltpu.VMEM((n_icol, ru_rows, 2 * width), f32),
+            pltpu.VMEM((n_icol, ru_rows + EXTRA, 2 * width), jnp.int16),
+            pltpu.VMEM((chips, ri_rows + EXTRA, 2 * width), jnp.int16),
+            pltpu.VMEM((n_icol, ru_rows + EXTRA, 2 * width), jnp.int16),
             pltpu.VMEM((slots, size, size), bf16),
             dma((4,)), dma, dma((slots,)),
             dma((n_icol,)), dma((n_icol,)), dma((chips,)), dma((chips,)),
@@ -212,6 +243,14 @@
         user_grad.reshape(ru_rows, width), item_grad.reshape(ri_rows, width),
         block_rows, block_cols, block_count, block_values.reshape(slots, size, size),
     )
+    un, in_, ub, ib, grads = pl.pallas_call(
+        hand_over,
+        out_shape=tuple(jax.ShapeDtypeStruct(r.shape, r.dtype) for r in results),
+        in_specs=[hbm] * len(results),
+        out_specs=(hbm,) * len(results),
+        scratch_shapes=[dma((len(results),))],
+        compiler_params=pltpu.CompilerParams(vmem_limit_bytes=63 * 1024 * 1024),
+    )(*results)
     return (
         un.reshape(1, ru_rows, width), in_.reshape(ri_rows, 1, width),
         ub.reshape(1, ru_rows, width), ib.reshape(ri_rows, 1, width),

time: 38.8 us -> 80 us (2.06)
  Pallas kernels: 28.8 us -> 78.5 us
  local copies, waits for them, and re-layouts: 8.34 us -> 0 us
    pallas_call x0 -> x1, Pallas kernels: none -> 54.8 us  [shards(): pl.pallas_call(hand_over, out_shape=tuple((jax.ShapeDtypeStruct(r.shape,...]
    unnamed x5 -> x0, local copies, waits for them, and re-layouts: 8.34 us -> none
    pallas_call x1, Pallas kernels: 28.8 us -> 23.7 us  [shards(): pl.pallas_call(functools.partial(kernel, n_urow, n_icol), out_shape=(jax....]
where the time goes in v2:
time: 80 us; the launch traced here: 79.8 us
  Pallas kernels  78.5 us (98%)
  between operations  1.29 us (2%)
    pallas_call x1, Pallas kernels, shards(): pl.pallas_call(hand_over, out_shape=tuple((jax.ShapeDtypeStruct(r.shape,...  54.8 us
    pallas_call x1, Pallas kernels, shards(): pl.pallas_call(functools.partial(kernel, n_urow, n_icol), out_shape=(jax....  23.7 us

profile of v2, /device:TPU:0, one launch (start us, length us, event | category | flops | bytes accessed | tf_op | source)
XLA Modules:
  0.0 79.8 jit_solution(10509919790569274113)
XLA Ops:
  1.3 23.7 %shard_map.119 = (bf16[256,128]{1,0:T(8,128)(2,1)}, bf16[128,128]{1,0:T(8,128)(2,1)}, bf16[256,128]{1,0:T(8,128)(2,1)}, bf16[128,128]{1,0:T(8,128)(2,1)}, bf16[12,256,256]{2,1,0:T(8,128)(2,1)}) custom-call(bf16[256,128]{1,0:T(8,128)(2,1)} %bitcast.11, bf16[128,128]{1,0:T(8,128)(2,1)} %bitcast.13, bf16[256,128]{1,0:T(8,128)(2,1)} %bitcast.12, ...), custom_call_target="tpu_custom_call" | custom-call | tf_op jit(solution)/shard_map/pallas_call | solution.py:208
  25.0 54.8 %shard_map.120 = (bf16[256,128]{1,0:T(8,128)(2,1)}, bf16[128,128]{1,0:T(8,128)(2,1)}, bf16[256,128]{1,0:T(8,128)(2,1)}, bf16[128,128]{1,0:T(8,128)(2,1)}, bf16[12,256,256]{2,1,0:T(8,128)(2,1)}) custom-call(bf16[256,128]{1,0:T(8,128)(2,1)} %get-tuple-element.15.refs_0_, bf16[128,128]{1,0:T(8,128)(2,1)} %get-tuple-element.16.refs_1_, ...), custom_call_target="tpu_custom_call" | custom-call | tf_op jit(solution)/shard_map/pallas_call | solution.py:246

commit v3 on v2

--- a/solution.py
+++ b/solution.py
@@ -31,11 +31,18 @@
 
 
 def hand_over(*refs):
-    half = (len(refs) - 1) // 2
-    copies = [pltpu.make_async_copy(refs[i], refs[half + i], refs[-1].at[i]) for i in range(half)]
-    for copy in copies:
-        copy.start()
-    for copy in copies:
+    given, taken, held, (in_sem, out_sem) = refs[:5], refs[5:10], refs[10:15], refs[15:]
+    slots = given[4].shape[0]
+    parts = [(given[i], held[i], taken[i]) for i in range(4)]
+    parts += [(given[4].at[k], held[4].at[k], taken[4].at[k]) for k in range(slots)]
+    loads = [pltpu.make_async_copy(p[0], p[1], in_sem.at[i]) for i, p in enumerate(parts)]
+    stores = [pltpu.make_async_copy(p[1], p[2], out_sem.at[i]) for i, p in enumerate(parts)]
+    for copy in loads:
+        copy.start()
+    for load, store in zip(loads, stores):
+        load.wait()
+        store.start()
+    for copy in stores:
         copy.wait()
 
 
@@ -248,7 +255,7 @@
         out_shape=tuple(jax.ShapeDtypeStruct(r.shape, r.dtype) for r in results),
         in_specs=[hbm] * len(results),
         out_specs=(hbm,) * len(results),
-        scratch_shapes=[dma((len(results),))],
+        scratch_shapes=[pltpu.VMEM(r.shape, r.dtype) for r in results] + [dma((slots + 4,)), dma((slots + 4,))],
         compiler_params=pltpu.CompilerParams(vmem_limit_bytes=63 * 1024 * 1024),
     )(*results)
     return (

time: 80 us -> 27.7 us (0.35)
  Pallas kernels: 78.5 us -> 26.2 us
    pallas_call x1, Pallas kernels: 54.8 us -> 2.49 us  [shards(): pl.pallas_call(hand_over, out_shape=tuple((jax.ShapeDtypeStruct(r.shape,...]
where the time goes in v3:
time: 27.7 us; the launch traced here: 27.5 us
  Pallas kernels  26.2 us (95%)
  between operations  1.29 us (5%)
    pallas_call x1, Pallas kernels, shards(): pl.pallas_call(functools.partial(kernel, n_urow, n_icol), out_shape=(jax....  23.7 us
    pallas_call x1, Pallas kernels, shards(): pl.pallas_call(hand_over, out_shape=tuple((jax.ShapeDtypeStruct(r.shape,...  2.49 us

profile of v3, /device:TPU:0, one launch (start us, length us, event | category | flops | bytes accessed | tf_op | source)
XLA Modules:
  0.0 27.5 jit_solution(375929098924515367)
XLA Ops:
  1.3 23.7 %shard_map.119 = (bf16[256,128]{1,0:T(8,128)(2,1)}, bf16[128,128]{1,0:T(8,128)(2,1)}, bf16[256,128]{1,0:T(8,128)(2,1)}, bf16[128,128]{1,0:T(8,128)(2,1)}, bf16[12,256,256]{2,1,0:T(8,128)(2,1)}) custom-call(bf16[256,128]{1,0:T(8,128)(2,1)} %bitcast.11, bf16[128,128]{1,0:T(8,128)(2,1)} %bitcast.13, bf16[256,128]{1,0:T(8,128)(2,1)} %bitcast.12, ...), custom_call_target="tpu_custom_call" | custom-call | tf_op jit(solution)/shard_map/pallas_call | solution.py:215
  25.0 2.5 %shard_map.120 = (bf16[256,128]{1,0:T(8,128)(2,1)}, bf16[128,128]{1,0:T(8,128)(2,1)}, bf16[256,128]{1,0:T(8,128)(2,1)}, bf16[128,128]{1,0:T(8,128)(2,1)}, bf16[12,256,256]{2,1,0:T(8,128)(2,1)}) custom-call(bf16[256,128]{1,0:T(8,128)(2,1)} %get-tuple-element.15.refs_0_, bf16[128,128]{1,0:T(8,128)(2,1)} %get-tuple-element.16.refs_1_, ...), custom_call_target="tpu_custom_call" | custom-call | tf_op jit(solution)/shard_map/pallas_call | solution.py:253

commit v4 on v2

--- a/solution.py
+++ b/solution.py
@@ -31,8 +31,8 @@
 
 
 def hand_over(*refs):
-    half = (len(refs) - 1) // 2
-    copies = [pltpu.make_async_copy(refs[i], refs[half + i], refs[-1].at[i]) for i in range(half)]
+    given, taken, sem = refs[:5], refs[5:10], refs[10]
+    copies = [pltpu.make_async_copy(given[i], taken[i], sem.at[i]) for i in range(5)]
     for copy in copies:
         copy.start()
     for copy in copies:
@@ -40,10 +40,10 @@
 
 
 def kernel(
-    n_urow, n_icol, users, items, user_grad, item_grad, rows, cols, count, values,
-    user_next, item_next, user_back, item_back, grads_out,
-    upair, ipair, blocks, dense, dense_t, upart, ipart, csum, pbuf, sbuf_u, rbuf_i, rbuf_u, grads,
-    local_sem, value_sem, grad_sem, su, ru, si, ri, sf, rf, sp, rp, sx, rx, sc, rc,
+    n_urow, n_icol, users, items, user_grad, item_grad, rows_in, cols_in, count_in, values,
+    user_next, item_next, user_back, item_back, grads,
+    upair, ipair, blocks, dense, dense_t, upart, ipart, csum, pbuf, sbuf_u, rbuf_i, rbuf_u, rows, cols, count,
+    local_sem, value_sem, index_sem, su, ru, si, ri, sf, rf, sp, rp, sx, rx, sc, rc,
 ):
     width = users.shape[1]
     ru_rows, ri_rows = users.shape[0], items.shape[0]
@@ -79,6 +79,13 @@
     chip_peers = [lax.rem(chip + o, chips) for o in range(1, chips)]
     icol_peers = [lax.rem(me_i + o, n_icol) for o in range(1, n_icol)]
 
+    barrier = pltpu.get_barrier_semaphore()
+    pl.semaphore_signal(barrier, inc=1, device_id={"urow": partner}, device_id_type=MESH)
+    for g in chip_peers:
+        pl.semaphore_signal(barrier, inc=1, device_id={"urow": 2 * g + core}, device_id_type=MESH)
+    for j in icol_peers:
+        pl.semaphore_signal(barrier, inc=1, device_id={"icol": j}, device_id_type=MESH)
+
     lo, hi = pl.ds(0, width), pl.ds(width, width)
     local = [
         pltpu.make_async_copy(items, ipair.at[(*in_pair(me_u, ri_rows), lo)], local_sem.at[0]),
@@ -90,13 +97,12 @@
         copy.start()
     value_copy = pltpu.make_async_copy(values, blocks, value_sem)
     value_copy.start()
-
-    barrier = pltpu.get_barrier_semaphore()
-    pl.semaphore_signal(barrier, inc=1, device_id={"urow": partner}, device_id_type=MESH)
-    for g in chip_peers:
-        pl.semaphore_signal(barrier, inc=1, device_id={"urow": 2 * g + core}, device_id_type=MESH)
-    for j in icol_peers:
-        pl.semaphore_signal(barrier, inc=1, device_id={"icol": j}, device_id_type=MESH)
+    index_copies = [
+        pltpu.make_async_copy(src, dst, index_sem.at[i])
+        for i, (src, dst) in enumerate([(rows_in, rows), (cols_in, cols), (count_in, count)])
+    ]
+    for copy in index_copies:
+        copy.start()
     pl.semaphore_wait(barrier, 1 + len(chip_peers) + len(icol_peers))
     for copy in local:
         copy.wait()
@@ -111,6 +117,8 @@
     for copy in sends:
         copy.start()
 
+    for copy in index_copies:
+        copy.wait()
     value_copy.wait()
     live_count = count[0, 0]
     for u in range(ub):
@@ -163,7 +171,6 @@
         copy.start()
         sends.append(copy)
 
-    writes = []
     for k in range(slots):
         left = upair[rows[0, 0, k]]
         right = ipair[cols[0, 0, k]]
@@ -172,9 +179,6 @@
             swap, right, (((1,), (1,)), ((), ())), preferred_element_type=jnp.float32
         )
         grads[k] = jnp.where(k < live_count, grad, 0.0).astype(jnp.bfloat16)
-        copy = pltpu.make_async_copy(grads.at[k], grads_out.at[k], grad_sem.at[k])
-        copy.start()
-        writes.append(copy)
 
     total = ipart[irows(me_u)] + pbuf[chip]
     for g in chip_peers:
@@ -188,8 +192,6 @@
         total = total + decode(rbuf_u.at[j])
     user_next[...] = total[:, :width].astype(jnp.bfloat16)
     user_back[...] = total[:, width:].astype(jnp.bfloat16)
-    for copy in writes:
-        copy.wait()
     for copy in sends:
         copy.wait_send()
 
@@ -201,21 +203,20 @@
     all_u, all_i = ru_rows * n_icol, ri_rows * n_urow
     chips = n_urow // 2
     bf16, f32 = jnp.bfloat16, jnp.float32
-    hbm = pl.BlockSpec(memory_space=pl.ANY)
-    smem = pl.BlockSpec(memory_space=pltpu.SMEM)
+    hbm = pl.BlockSpec(memory_space=pltpu.HBM)
     vmem = pl.BlockSpec(memory_space=pltpu.VMEM)
     dma = pltpu.SemaphoreType.DMA
     results = pl.pallas_call(
         functools.partial(kernel, n_urow, n_icol),
         out_shape=(
-            jax.ShapeDtypeStruct((ru_rows, width), bf16),
-            jax.ShapeDtypeStruct((ri_rows, width), bf16),
-            jax.ShapeDtypeStruct((ru_rows, width), bf16),
-            jax.ShapeDtypeStruct((ri_rows, width), bf16),
-            jax.ShapeDtypeStruct((slots, size, size), bf16),
+            pltpu.VMEM((ru_rows, width), bf16),
+            pltpu.VMEM((ri_rows, width), bf16),
+            pltpu.VMEM((ru_rows, width), bf16),
+            pltpu.VMEM((ri_rows, width), bf16),
+            pltpu.VMEM((slots, size, size), bf16),
         ),
-        in_specs=[hbm] * 4 + [smem] * 3 + [hbm],
-        out_specs=(vmem, vmem, vmem, vmem, hbm),
+        in_specs=[hbm] * 8,
+        out_specs=(vmem,) * 5,
         scratch_shapes=[
             pltpu.VMEM((all_u // size, size, 2 * width), bf16),
             pltpu.VMEM((all_i // size, size, 2 * width), bf16),
@@ -229,14 +230,15 @@
             pltpu.VMEM((n_icol, ru_rows + EXTRA, 2 * width), jnp.int16),
             pltpu.VMEM((chips, ri_rows + EXTRA, 2 * width), jnp.int16),
             pltpu.VMEM((n_icol, ru_rows + EXTRA, 2 * width), jnp.int16),
-            pltpu.VMEM((slots, size, size), bf16),
-            dma((4,)), dma, dma((slots,)),
+            pltpu.SMEM(block_rows.shape, jnp.int32), pltpu.SMEM(block_cols.shape, jnp.int32),
+            pltpu.SMEM(block_count.shape, jnp.int32),
+            dma((4,)), dma, dma((3,)),
             dma((n_icol,)), dma((n_icol,)), dma((chips,)), dma((chips,)),
             dma((chips,)), dma((chips,)), dma((chips,)), dma((chips,)),
             dma((n_icol,)), dma((n_icol,)), dma((chips,)), dma((chips,)),
         ],
         compiler_params=pltpu.CompilerParams(
-            collective_id=0, has_side_effects=True, vmem_limit_bytes=63 * 1024 * 1024
+            collective_id=0, has_side_effects=True, vmem_limit_bytes=62 * 1024 * 1024
         ),
     )(
         users.reshape(ru_rows, width), items.reshape(ri_rows, width),
@@ -246,10 +248,9 @@
     un, in_, ub, ib, grads = pl.pallas_call(
         hand_over,
         out_shape=tuple(jax.ShapeDtypeStruct(r.shape, r.dtype) for r in results),
-        in_specs=[hbm] * len(results),
+        in_specs=[vmem] * len(results),
         out_specs=(hbm,) * len(results),
         scratch_shapes=[dma((len(results),))],
-        compiler_params=pltpu.CompilerParams(vmem_limit_bytes=63 * 1024 * 1024),
     )(*results)
     return (
         un.reshape(1, ru_rows, width), in_.reshape(ri_rows, 1, width),

time: 80 us -> 30.2 us (0.38)
  Pallas kernels: 78.5 us -> 25.1 us
  local copies, waits for them, and re-layouts: 0 us -> 3.61 us
    pallas_call x1, Pallas kernels: 54.8 us -> 2.77 us  [shards(): pl.pallas_call(hand_over, out_shape=tuple((jax.ShapeDtypeStruct(r.shape,...]
    unnamed x0 -> x10, local copies, waits for them, and re-layouts: none -> 3.61 us
    pallas_call x1, Pallas kernels: 23.7 us -> 22.3 us  [shards(): pl.pallas_call(functools.partial(kernel, n_urow, n_icol), out_shape=(pltp...]
where the time goes in v4:
time: 30.2 us; the launch traced here: 30 us
  Pallas kernels  25.1 us (83%)
  local copies, waits for them, and re-layouts  3.61 us (12%)
  between operations  1.3 us (4%)
    pallas_call x1, Pallas kernels, shards(): pl.pallas_call(functools.partial(kernel, n_urow, n_icol), out_shape=(pltp...  22.3 us
    unnamed x10, local copies, waits for them, and re-layouts  3.61 us
    pallas_call x1, Pallas kernels, shards(): pl.pallas_call(hand_over, out_shape=tuple((jax.ShapeDtypeStruct(r.shape,...  2.77 us

profile of v4, /device:TPU:0, one launch (start us, length us, event | category | flops | bytes accessed | tf_op | source)
XLA Modules:
  0.0 30.0 jit_solution(2950638669706396386)
XLA Ops:
  1.3 22.3 %shard_map.119 = (bf16[256,128]{1,0:T(8,128)(2,1)S(1)}, bf16[128,128]{1,0:T(8,128)(2,1)S(1)}, bf16[256,128]{1,0:T(8,128)(2,1)S(1)}, bf16[128,128]{1,0:T(8,128)(2,1)S(1)}, bf16[12,256,256]{2,1,0:T(8,128)(2,1)S(1)}) custom-call(bf16[256,128]{1,0:T(8,128)(2,1)} %bitcast.11, bf16[128,128]{1,0:T(8,128)(2,1)} %bitcast.13, bf16[256,128]{1,0:T(8,128)(2,1)} %bitcast.12, ...), custom_call_target="tpu_custom_call" | custom-call | tf_op jit(solution)/shard_map/pallas_call | solution.py:209
  23.6 0.0 copy-start
  23.6 1.1 %copy-done = bf16[12,256,256]{2,1,0:T(8,128)(2,1)} copy-done((bf16[12,256,256]{2,1,0:T(8,128)(2,1)}, bf16[12,256,256]{2,1,0:T(8,128)(2,1)S(1)}, u32[]{:S(2)}) %copy-start) | copy-done | bytes 1572888
  24.8 0.0 copy-start.1
  24.8 0.6 %copy-done.1 = bf16[256,128]{1,0:T(8,128)(2,1)} copy-done((bf16[256,128]{1,0:T(8,128)(2,1)}, bf16[256,128]{1,0:T(8,128)(2,1)S(1)}, u32[]{:S(2)}) %copy-start.1) | copy-done | bytes 65560
  25.4 0.0 copy-start.2
  25.4 0.6 %copy-done.2 = bf16[256,128]{1,0:T(8,128)(2,1)} copy-done((bf16[256,128]{1,0:T(8,128)(2,1)}, bf16[256,128]{1,0:T(8,128)(2,1)S(1)}, u32[]{:S(2)}) %copy-start.2) | copy-done | bytes 65560
  26.0 0.0 copy-start.3
  26.0 0.6 %copy-done.3 = bf16[128,128]{1,0:T(8,128)(2,1)} copy-done((bf16[128,128]{1,0:T(8,128)(2,1)}, bf16[128,128]{1,0:T(8,128)(2,1)S(1)}, u32[]{:S(2)}) %copy-start.3) | copy-done | bytes 32792
  26.6 0.0 copy-start.4
  26.6 0.6 %copy-done.4 = bf16[128,128]{1,0:T(8,128)(2,1)} copy-done((bf16[128,128]{1,0:T(8,128)(2,1)}, bf16[128,128]{1,0:T(8,128)(2,1)S(1)}, u32[]{:S(2)}) %copy-start.4) | copy-done | bytes 32792
  27.2 2.8 %shard_map.120 = (bf16[256,128]{1,0:T(8,128)(2,1)}, bf16[128,128]{1,0:T(8,128)(2,1)}, bf16[256,128]{1,0:T(8,128)(2,1)}, bf16[128,128]{1,0:T(8,128)(2,1)}, bf16[12,256,256]{2,1,0:T(8,128)(2,1)}) custom-call(bf16[256,128]{1,0:T(8,128)(2,1)} %copy-done.1, bf16[128,128]{1,0:T(8,128)(2,1)} %copy-done.3, bf16[256,128]{1,0:T(8,128)(2,1)} %copy-done.2, ...), custom_call_target="tpu_custom_call" | custom-call | tf_op jit(solution)/shard_map/pallas_call | solution.py:248
Async XLA Ops:
  23.6 1.2 %copy-start = (bf16[12,256,256]{2,1,0:T(8,128)(2,1)}, bf16[12,256,256]{2,1,0:T(8,128)(2,1)S(1)}, u32[]{:S(2)}) copy-start(bf16[12,256,256]{2,1,0:T(8,128)(2,1)S(1)} %get-tuple-element.19.refs_4_) | copy-start | bytes 4718596
  24.8 0.6 %copy-start.1 = (bf16[256,128]{1,0:T(8,128)(2,1)}, bf16[256,128]{1,0:T(8,128)(2,1)S(1)}, u32[]{:S(2)}) copy-start(bf16[256,128]{1,0:T(8,128)(2,1)S(1)} %get-tuple-element.15.refs_0_) | copy-start | bytes 196612
  25.4 0.6 %copy-start.2 = (bf16[256,128]{1,0:T(8,128)(2,1)}, bf16[256,128]{1,0:T(8,128)(2,1)S(1)}, u32[]{:S(2)}) copy-start(bf16[256,128]{1,0:T(8,128)(2,1)S(1)} %get-tuple-element.17.refs_2_) | copy-start | bytes 196612
  26.0 0.6 %copy-start.3 = (bf16[128,128]{1,0:T(8,128)(2,1)}, bf16[128,128]{1,0:T(8,128)(2,1)S(1)}, u32[]{:S(2)}) copy-start(bf16[128,128]{1,0:T(8,128)(2,1)S(1)} %get-tuple-element.16.refs_1_) | copy-start | bytes 98308
  26.6 0.6 %copy-start.4 = (bf16[128,128]{1,0:T(8,128)(2,1)}, bf16[128,128]{1,0:T(8,128)(2,1)S(1)}, u32[]{:S(2)}) copy-start(bf16[128,128]{1,0:T(8,128)(2,1)S(1)} %get-tuple-element.18.refs_3_) | copy-start | bytes 98308

commit v5 on v4

--- a/solution.py
+++ b/solution.py
@@ -40,9 +40,9 @@
 
 
 def kernel(
-    n_urow, n_icol, users, items, user_grad, item_grad, rows_in, cols_in, count_in, values,
+    n_urow, n_icol, users, items, user_grad, item_grad, rows_in, cols_in, count, values,
     user_next, item_next, user_back, item_back, grads,
-    upair, ipair, blocks, dense, dense_t, upart, ipart, csum, pbuf, sbuf_u, rbuf_i, rbuf_u, rows, cols, count,
+    upair, ipair, blocks, dense, dense_t, upart, ipart, csum, pbuf, sbuf_u, rbuf_i, rbuf_u, rows, cols,
     local_sem, value_sem, index_sem, su, ru, si, ri, sf, rf, sp, rp, sx, rx, sc, rc,
 ):
     width = users.shape[1]
@@ -99,7 +99,7 @@
     value_copy.start()
     index_copies = [
         pltpu.make_async_copy(src, dst, index_sem.at[i])
-        for i, (src, dst) in enumerate([(rows_in, rows), (cols_in, cols), (count_in, count)])
+        for i, (src, dst) in enumerate([(rows_in, rows), (cols_in, cols)])
     ]
     for copy in index_copies:
         copy.start()
@@ -215,7 +215,7 @@
             pltpu.VMEM((ri_rows, width), bf16),
             pltpu.VMEM((slots, size, size), bf16),
         ),
-        in_specs=[hbm] * 8,
+        in_specs=[hbm] * 6 + [pl.BlockSpec(memory_space=pltpu.SMEM), hbm],
         out_specs=(vmem,) * 5,
         scratch_shapes=[
             pltpu.VMEM((all_u // size, size, 2 * width), bf16),
@@ -231,8 +231,7 @@
             pltpu.VMEM((chips, ri_rows + EXTRA, 2 * width), jnp.int16),
             pltpu.VMEM((n_icol, ru_rows + EXTRA, 2 * width), jnp.int16),
             pltpu.SMEM(block_rows.shape, jnp.int32), pltpu.SMEM(block_cols.shape, jnp.int32),
-            pltpu.SMEM(block_count.shape, jnp.int32),
-            dma((4,)), dma, dma((3,)),
+            dma((4,)), dma, dma((2,)),
             dma((n_icol,)), dma((n_icol,)), dma((chips,)), dma((chips,)),
             dma((chips,)), dma((chips,)), dma((chips,)), dma((chips,)),
             dma((n_icol,)), dma((n_icol,)), dma((chips,)), dma((chips,)),
@@ -251,6 +250,7 @@
         in_specs=[vmem] * len(results),
         out_specs=(hbm,) * len(results),
         scratch_shapes=[dma((len(results),))],
+        compiler_params=pltpu.CompilerParams(vmem_limit_bytes=1024 * 1024),
     )(*results)
     return (
         un.reshape(1, ru_rows, width), in_.reshape(ri_rows, 1, width),

time: 30.2 us -> 24.9 us (0.82)
  local copies, waits for them, and re-layouts: 3.61 us -> 0 us
  Pallas kernels: 25.1 us -> 23.5 us
    unnamed x10 -> x0, local copies, waits for them, and re-layouts: 3.61 us -> none
    pallas_call x1, Pallas kernels: 2.77 us -> 1.25 us  [shards(): pl.pallas_call(hand_over, out_shape=tuple((jax.ShapeDtypeStruct(r.shape,...]
where the time goes in v5:
time: 24.9 us; the launch traced here: 24.8 us
  Pallas kernels  23.5 us (94%)
  between operations  1.29 us (5%)
    pallas_call x1, Pallas kernels, shards(): pl.pallas_call(functools.partial(kernel, n_urow, n_icol), out_shape=(pltp...  22.2 us
    pallas_call x1, Pallas kernels, shards(): pl.pallas_call(hand_over, out_shape=tuple((jax.ShapeDtypeStruct(r.shape,...  1.25 us

profile of v5, /device:TPU:0, one launch (start us, length us, event | category | flops | bytes accessed | tf_op | source)
XLA Modules:
  0.0 24.8 jit_solution(13484159833022977602)
XLA Ops:
  1.3 22.2 %shard_map.119 = (bf16[256,128]{1,0:T(8,128)(2,1)S(1)}, bf16[128,128]{1,0:T(8,128)(2,1)S(1)}, bf16[256,128]{1,0:T(8,128)(2,1)S(1)}, bf16[128,128]{1,0:T(8,128)(2,1)S(1)}, bf16[12,256,256]{2,1,0:T(8,128)(2,1)S(1)}) custom-call(bf16[256,128]{1,0:T(8,128)(2,1)} %bitcast.11, bf16[128,128]{1,0:T(8,128)(2,1)} %bitcast.13, bf16[256,128]{1,0:T(8,128)(2,1)} %bitcast.12, ...), custom_call_target="tpu_custom_call" | custom-call | tf_op jit(solution)/shard_map/pallas_call | solution.py:209
  23.5 1.3 %shard_map.120 = (bf16[256,128]{1,0:T(8,128)(2,1)}, bf16[128,128]{1,0:T(8,128)(2,1)}, bf16[256,128]{1,0:T(8,128)(2,1)}, bf16[128,128]{1,0:T(8,128)(2,1)}, bf16[12,256,256]{2,1,0:T(8,128)(2,1)}) custom-call(bf16[256,128]{1,0:T(8,128)(2,1)S(1)} %get-tuple-element.15.refs_0_, bf16[128,128]{1,0:T(8,128)(2,1)S(1)} %get-tuple-element.16.refs_1_, ...), custom_call_target="tpu_custom_call" | custom-call | tf_op jit(solution)/shard_map/pallas_call | solution.py:247

commit v6 on v5

--- a/solution.py
+++ b/solution.py
@@ -141,10 +141,11 @@
 
     for j in icol_peers:
         remote(mine_u, upart_of(j), su.at[j], ru.at[j], {"icol": j}).wait_recv()
-    for c in range(ib):
-        at = slice(c * size, (c + 1) * size)
-        ipart[at] = jnp.dot(dense_t[at], upair[...].reshape(-1, 2 * width), preferred_element_type=jnp.float32)
     for g in chip_peers + [chip]:
+        at = pl.ds(pl.multiple_of(g * 2 * ri_rows, 2 * ri_rows), 2 * ri_rows)
+        ipart[at] = jnp.dot(
+            dense_t[at], upair[...].reshape(-1, 2 * width), preferred_element_type=jnp.float32
+        )
         copy = remote(
             ipart.at[irows(2 * g + 1 - core)], pbuf.at[g], sp.at[g], rp.at[g], {"urow": partner}
         )
@@ -154,22 +155,28 @@
     for g in [chip] + chip_peers:
         there = ipart_of(2 * g + 1 - core)
         remote(there, there, sf.at[g], rf.at[g], {"urow": partner}).wait_recv()
-    for u in range(ub):
-        at = slice(u * size, (u + 1) * size)
-        upart[at] = jnp.dot(dense[at], ipair[...].reshape(-1, 2 * width), preferred_element_type=jnp.float32)
-    for j in icol_peers:
-        encode(upart[urows(j)], sbuf_u.at[j])
-        copy = remote(sbuf_u.at[j], rbuf_u.at[me_i], sx.at[j], rx.at[me_i], {"icol": j})
-        copy.start()
-        sends.append(copy)
-
-    for g in chip_peers + [chip]:
-        remote(pbuf.at[g], pbuf.at[g], sp.at[g], rp.at[g], {"urow": partner}).wait_recv()
-    for g in chip_peers:
-        encode(ipart[irows(2 * g + core)] + pbuf[g], csum.at[g])
-        copy = remote(csum.at[g], rbuf_i.at[chip], sc.at[g], rc.at[chip], {"urow": 2 * g + core})
-        copy.start()
-        sends.append(copy)
+
+    def user_sums(j):
+        return jnp.dot(
+            dense[urows(j)], ipair[...].reshape(-1, 2 * width), preferred_element_type=jnp.float32
+        )
+
+    for o in range(max(len(icol_peers), len(chip_peers))):
+        if o < len(icol_peers):
+            j = icol_peers[o]
+            encode(user_sums(j), sbuf_u.at[j])
+            copy = remote(sbuf_u.at[j], rbuf_u.at[me_i], sx.at[j], rx.at[me_i], {"icol": j})
+            copy.start()
+            sends.append(copy)
+        if o < len(chip_peers):
+            g = chip_peers[o]
+            remote(pbuf.at[g], pbuf.at[g], sp.at[g], rp.at[g], {"urow": partner}).wait_recv()
+            encode(ipart[irows(2 * g + core)] + pbuf[g], csum.at[g])
+            copy = remote(csum.at[g], rbuf_i.at[chip], sc.at[g], rc.at[chip], {"urow": 2 * g + core})
+            copy.start()
+            sends.append(copy)
+    remote(pbuf.at[chip], pbuf.at[chip], sp.at[chip], rp.at[chip], {"urow": partner}).wait_recv()
+    upart[...] = user_sums(me_i)
 
     for k in range(slots):
         left = upair[rows[0, 0, k]]
@@ -186,7 +193,7 @@
         total = total + decode(rbuf_i.at[g])
     item_next[...] = total[:, :width].astype(jnp.bfloat16)
     item_back[...] = total[:, width:].astype(jnp.bfloat16)
-    total = upart[urows(me_i)]
+    total = upart[...]
     for j in icol_peers:
         remote(sbuf_u.at[j], rbuf_u.at[j], sx.at[j], rx.at[j], {"icol": j}).wait_recv()
         total = total + decode(rbuf_u.at[j])
@@ -223,7 +230,7 @@
             pltpu.VMEM((slots, size, size), bf16),
             pltpu.VMEM((all_u, all_i), bf16),
             pltpu.VMEM((all_i, all_u), bf16),
-            pltpu.VMEM((all_u, 2 * width), f32),
+            pltpu.VMEM((ru_rows, 2 * width), f32),
             pltpu.VMEM((all_i, 2 * width), f32),
             pltpu.VMEM((chips, ri_rows + EXTRA, 2 * width), jnp.int16),
             pltpu.VMEM((chips, ri_rows, 2 * width), f32),

time: 24.9 us -> 25.7 us (1.032)
  Pallas kernels: 23.5 us -> 24.2 us
    pallas_call x1, Pallas kernels: 22.2 us -> 23 us  [shards(): pl.pallas_call(functools.partial(kernel, n_urow, n_icol), out_shape=(pltp...]
where the time goes in v6:
time: 25.7 us; the launch traced here: 25.5 us
  Pallas kernels  24.2 us (94%)
  between operations  1.29 us (5%)
    pallas_call x1, Pallas kernels, shards(): pl.pallas_call(functools.partial(kernel, n_urow, n_icol), out_shape=(pltp...  23 us
    pallas_call x1, Pallas kernels, shards(): pl.pallas_call(hand_over, out_shape=tuple((jax.ShapeDtypeStruct(r.shape,...  1.25 us

profile of v6, /device:TPU:0, one launch (start us, length us, event | category | flops | bytes accessed | tf_op | source)
XLA Modules:
  0.0 25.5 jit_solution(17247879160734880255)
XLA Ops:
  1.3 23.0 %shard_map.119 = (bf16[256,128]{1,0:T(8,128)(2,1)S(1)}, bf16[128,128]{1,0:T(8,128)(2,1)S(1)}, bf16[256,128]{1,0:T(8,128)(2,1)S(1)}, bf16[128,128]{1,0:T(8,128)(2,1)S(1)}, bf16[12,256,256]{2,1,0:T(8,128)(2,1)S(1)}) custom-call(bf16[256,128]{1,0:T(8,128)(2,1)} %bitcast.11, bf16[128,128]{1,0:T(8,128)(2,1)} %bitcast.13, bf16[256,128]{1,0:T(8,128)(2,1)} %bitcast.12, ...), custom_call_target="tpu_custom_call" | custom-call | tf_op jit(solution)/shard_map/pallas_call | solution.py:216
  24.3 1.3 %shard_map.120 = (bf16[256,128]{1,0:T(8,128)(2,1)}, bf16[128,128]{1,0:T(8,128)(2,1)}, bf16[256,128]{1,0:T(8,128)(2,1)}, bf16[128,128]{1,0:T(8,128)(2,1)}, bf16[12,256,256]{2,1,0:T(8,128)(2,1)}) custom-call(bf16[256,128]{1,0:T(8,128)(2,1)S(1)} %get-tuple-element.15.refs_0_, bf16[128,128]{1,0:T(8,128)(2,1)S(1)} %get-tuple-element.16.refs_1_, ...), custom_call_target="tpu_custom_call" | custom-call | tf_op jit(solution)/shard_map/pallas_call | solution.py:254
